TPU v7x, 256 devices: a whole 4x4x8 slice. The times are simulated.
256 devices in a mesh: group: 8 (over y, z_hi), ctx: 32 (over x, z_lo, core).
Axes of the slice: x: 4, y: 4, z: 8 (z_hi: 2, z_lo: 4; z = z_hi * 4 + z_lo), core: 2. Of those that a mesh axis runs over, the one named last changes fastest.
Arguments:
- queries: bfloat16 [2048, 5120], P(('group', 'ctx')), may hold values from -10 to 10
- grad_out: bfloat16 [2048, 5120], P(('group', 'ctx')), may hold values from -6 to 6
- keys: bfloat16 [16384, 1024], P('ctx'), may hold values from -6 to 6
- values: bfloat16 [16384, 1024], P('ctx'), may hold values from -6 to 6
- prompt_len: int32 [1], replicated, may hold values from 16128 to 16384
- resp_len: int32 [8, 2], P('group'), may hold values from 64 to 128
Outputs:
- query_grad: bfloat16 [2048, 5120], P(('group', 'ctx'))
- key_grad: bfloat16 [16384, 1024], P('ctx', 'group')
- value_grad: bfloat16 [16384, 1024], P('ctx', 'group')
All inputs are finite; a program needn't handle non-finite values.
Results may differ from a plain program's by a relative error of at most 0.018.
Values may be sent and summed in bfloat16 or wider, within the bound.
A program may use at most 64 MiB of HBM per device.

v0:
```python
import jax
import jax.numpy as jnp
from jax import lax
from jax.sharding import PartitionSpec as P

QH = 40
KH = 8
HD = 128
RESP = 2
WINDOW = 128


def merged(value, axis, join):
    pieces = jax.tree.map(lambda part: lax.all_gather(part, axis), value)
    head = jax.tree.map(lambda part: part[0], pieces)
    tail = jax.tree.map(lambda part: part[1:], pieces)
    running, _ = lax.scan(lambda running, slab: (join(running, slab), None), head, tail)
    return running


def combine_pair(first, second):
    top = jnp.maximum(first[0], second[0])
    return (top, first[1] * jnp.exp(first[0] - top) + second[1] * jnp.exp(second[0] - top))


def on_device(queries, grad_out, keys, values, prompt_len, resp_len):
    share = QH // KH
    scale = 1.0 / HD**0.5
    whole_q, whole_do = (
        lax.all_gather(queries, "ctx", axis=0, tiled=True),
        lax.all_gather(grad_out, "ctx", axis=0, tiled=True),
    )
    rows_all = whole_q.shape[0]
    span = keys.shape[0]
    rows = jnp.arange(rows_all, dtype=jnp.int32)
    picks = jnp.arange(RESP, dtype=jnp.int32)
    limit = jnp.sum(
        jnp.where((rows // WINDOW)[:, None] == picks[None, :], resp_len[0][None, :], 0), axis=1
    )
    live = rows % WINDOW < limit
    masked = jnp.where(live[:, None], whole_do, jnp.zeros_like(whole_do))
    first_key = lax.axis_index("ctx") * span
    key_ok = first_key + jnp.arange(span, dtype=jnp.int32) < prompt_len[0]

    def pieces(head):
        q_head = lax.dynamic_slice_in_dim(whole_q, head * share * HD, share * HD, 1).reshape(
            rows_all, share, HD
        )
        do_head = lax.dynamic_slice_in_dim(masked, head * share * HD, share * HD, 1).reshape(
            rows_all, share, HD
        )
        k_head = lax.dynamic_slice_in_dim(keys, head * HD, HD, 1)
        v_head = lax.dynamic_slice_in_dim(values, head * HD, HD, 1)
        return (q_head, do_head, k_head, v_head)

    def scores_of(q_head, k_head):
        scores = (
            jnp.einsum("rgd,kd->grk", q_head, k_head, preferred_element_type=jnp.float32) * scale
        )
        return jnp.where(key_ok[None, None, :], scores, jnp.float32(-1e30))

    def dprobs_of(do_head, v_head):
        return jnp.einsum("rgd,kd->grk", do_head, v_head, preferred_element_type=jnp.float32)

    heads = jnp.arange(KH, dtype=jnp.int32)

    def local_stats(head):
        q_head, do_head, k_head, v_head = pieces(head)
        scores = scores_of(q_head, k_head)
        top = jnp.max(scores, axis=-1)
        return (top, jnp.sum(jnp.exp(scores - top[..., None]), axis=-1))

    top_loc, total_loc = lax.map(local_stats, heads)
    top_all, total_all = merged((top_loc, total_loc), "ctx", combine_pair)

    def local_dot(head):
        q_head, do_head, k_head, v_head = pieces(head)
        scores = scores_of(q_head, k_head)
        probs = jnp.exp(scores - top_all[head][..., None]) / total_all[head][..., None]
        return jnp.sum(probs * dprobs_of(do_head, v_head), axis=-1)

    row_dot = lax.psum(lax.map(local_dot, heads), "ctx")

    def grads_step(head, carry):
        dq_acc, dk_acc, dv_acc = carry
        q_head, do_head, k_head, v_head = pieces(head)
        scores = scores_of(q_head, k_head)
        probs = jnp.exp(scores - top_all[head][..., None]) / total_all[head][..., None]
        dprobs = dprobs_of(do_head, v_head)
        dscores = (probs * (dprobs - row_dot[head][..., None]) * scale).astype(jnp.bfloat16)
        probs_low = probs.astype(jnp.bfloat16)
        dq = jnp.einsum("grk,kd->rgd", dscores, k_head, preferred_element_type=jnp.float32).reshape(
            rows_all, share * HD
        )
        dk = jnp.einsum("grk,rgd->kd", dscores, q_head, preferred_element_type=jnp.float32)
        dv = jnp.einsum("grk,rgd->kd", probs_low, do_head, preferred_element_type=jnp.float32)
        dq_acc = lax.dynamic_update_slice_in_dim(dq_acc, dq, head * share * HD, 1)
        dk_acc = lax.dynamic_update_slice_in_dim(dk_acc, dk, head * HD, 1)
        dv_acc = lax.dynamic_update_slice_in_dim(dv_acc, dv, head * HD, 1)
        return (dq_acc, dk_acc, dv_acc)

    start = (
        jnp.zeros((rows_all, QH * HD), jnp.float32),
        jnp.zeros((span, KH * HD), jnp.float32),
        jnp.zeros((span, KH * HD), jnp.float32),
    )
    dq_term, dk_term, dv_term = lax.fori_loop(0, KH, grads_step, start)
    query_grad = lax.psum_scatter(dq_term, "ctx", scatter_dimension=0, tiled=True).astype(
        jnp.bfloat16
    )
    key_sum = lax.psum_scatter(dk_term, "group", scatter_dimension=1, tiled=True)
    value_sum = lax.psum_scatter(dv_term, "group", scatter_dimension=1, tiled=True)
    key_grad = key_sum.astype(jnp.bfloat16)
    value_grad = value_sum.astype(jnp.bfloat16)
    return (query_grad, key_grad, value_grad)


def solution(mesh):
    in_specs = (
        P(("group", "ctx"), None),
        P(("group", "ctx"), None),
        P("ctx", None),
        P("ctx", None),
        P(),
        P("group", None),
    )
    out_specs = (P(("group", "ctx"), None), P("ctx", "group"), P("ctx", "group"))
    return jax.shard_map(
        on_device, mesh=mesh, in_specs=in_specs, out_specs=out_specs, check_vma=False
    )
```

profile of v0, /device:TPU:1, one launch (start us, length us, event | category | flops | bytes accessed | tf_op | source)
XLA Modules:
  0.0 902.5 jit_solution(16251579187241545967)
XLA Ops:
  8.7 66.3 %all-gather.7.cloned.1.call-done = bf16[256,5120]{1,0:T(8,128)(2,1)} async-done(((bf16[8,5120]{1,0:T(8,128)(2,1)}), bf16[256,5120]{1,0:T(8,128)(2,1)}) %all-gather.7.cloned.1.call-update) | async-done | bytes 2621456 | tf_op jit(solution)/shard_map/all_gather | solution.py:30
  75.0 4.4 copy.63
  79.4 57.1 %while.61 = (s32[]{:T(128)}, f32[8,5,256]{2,0,1:T(8,128)S(1)}, f32[8,5,256]{2,0,1:T(8,128)}, s32[8]{0:T(128)S(1)}, bf16[512,1024]{1,0:T(8,128)(2,1)}, /*index=5*...) while((s32[]{:T(128)}, f32[8,5,256]{2,0,1:T(8,128)S(1)}, ...), condition=%wide.region_4.5_spmd.clone, body=%wide.region_1.4_spmd.clone.sunk | while | flops 172358160 | bytes 6415117 | solution.py:73
  83.0 1.5 bitcast_reduce_fusion.2
  85.1 1.4 dynamic_update_slice.66
  90.1 1.5 bitcast_reduce_fusion.2
  92.2 1.4 dynamic_update_slice.66
  97.2 1.5 bitcast_reduce_fusion.2
  99.4 1.4 dynamic_update_slice.66
  104.4 1.5 bitcast_reduce_fusion.2
  106.5 1.4 dynamic_update_slice.66
  111.5 1.5 bitcast_reduce_fusion.2
  113.7 1.4 dynamic_update_slice.66
  118.6 1.5 bitcast_reduce_fusion.2
  120.8 1.4 dynamic_update_slice.66
  125.8 1.5 bitcast_reduce_fusion.2
  127.9 1.4 dynamic_update_slice.66
  132.9 1.5 bitcast_reduce_fusion.2
  135.1 1.4 dynamic_update_slice.66
  137.9 2.0 broadcast_select_fusion
  139.9 2.6 copy.64
  142.5 55.2 %all-gather.11.cloned.1.call-done = f32[256,5,256]{2,0,1:T(8,128)} async-done(((f32[8,5,256]{2,0,1:T(8,128)}), f32[256,5,256]{2,0,1:T(8,128)}) %all-gather.11.cloned.1.call-update) | async-done | bytes 1310736 | tf_op jit(solution)/shard_map/all_gather | solution.py:14
  198.6 59.8 %all-gather.13.cloned.1.call-done = f32[256,5,256]{2,0,1:T(8,128)} async-done(((f32[8,5,256]{2,0,1:T(8,128)}), f32[256,5,256]{2,0,1:T(8,128)}) %all-gather.13.cloned.1.call-update) | async-done | bytes 1310736 | tf_op jit(solution)/shard_map/all_gather | solution.py:14
  259.3 1.4 slice_bitcast_fusion.1
  260.8 3.6 while.60
  264.4 71.3 %while.62 = (s32[]{:T(128)}, f32[8,5,256]{2,1,0:T(8,128)S(1)}, s32[8]{0:T(128)S(1)}, bf16[512,1024]{1,0:T(8,128)(2,1)}, bf16[256,5120]{0,1:T(8,128)(2,1)}, /*ind...) while((s32[]{:T(128)}, f32[8,5,256]{2,1,0:T(8,128)S(1)}, ...), condition=%wide.region_9.10_spmd.clone, body=%wide.region_7.9_spmd.clone.sunk | while | flops 339476224 | bytes 7524691 | solution.py:82
  270.0 1.4 fusion.95
  271.4 1.8 fusion.96
  279.0 1.4 fusion.95
  280.3 1.8 fusion.96
  289.3 1.8 fusion.96
  296.8 1.4 fusion.95
  298.2 1.8 fusion.96
  307.1 1.8 fusion.96
  316.0 1.8 fusion.96
  324.9 1.8 fusion.96
  333.8 1.8 fusion.96
  335.7 130.0 %psum.7 = f32[8,5,256]{2,1,0:T(8,128)S(1)} all-reduce(f32[8,5,256]{2,1,0:T(8,128)S(1)} %get-tuple-element.538), channel_id=1, replica_groups=mesh['group'=8,'ctx'=32] {'ctx'}, use_global_device_ids=true, to_apply=%region_10.11 | all-reduce | flops 10240 | bytes 81920 | tf_op jit(solution)/shard_map/psum | solution.py:82
  465.7 1.6 broadcast.99.clone
  467.3 1.6 broadcast.99
  468.9 2.9 broadcast_in_dim.114.clone
  471.8 78.4 %while.63 = (s32[]{:T(128)}, f32[256,5120]{1,0:T(8,128)}, f32[512,1024]{1,0:T(8,128)}, f32[512,1024]{1,0:T(8,128)}, bf16[512,1024]{1,0:T(8,128)(2,1)}, /*index=5...) while((s32[]{:T(128)}, f32[256,5120]{1,0:T(8,128)}, ...), condition=%wide.region_12.13_spmd.clone, body=%wide.region_11.12_spmd.clone.sunk | while | flops 844760064 | bytes 18659644 | solution.py:107
  473.6 1.7 fusion.107
  475.3 1.4 fusion.108
  483.4 1.7 fusion.107
  485.1 1.4 fusion.108
  493.3 1.7 fusion.107
  494.9 1.4 fusion.108
  503.0 1.7 fusion.107
  504.7 1.4 fusion.108
  512.9 1.7 fusion.107
  514.5 1.4 fusion.108
  522.7 1.7 fusion.107
  524.4 1.4 fusion.108
  532.5 1.7 fusion.107
  534.1 1.4 fusion.108
  542.2 1.7 fusion.107
  543.9 1.4 fusion.108
  551.6 96.0 %reduce-scatter.8.cloned.1.call-done = f32[512,128]{1,0:T(8,128)} async-done(((f32[512,1024]{1,0:T(8,128)}), f32[512,128]{1,0:T(8,128)}) %reduce-scatter.8.cloned.1.call-update) | async-done | bytes 262160 | tf_op jit(solution)/shard_map/reduce_scatter | solution.py:112
  647.6 1.6 convert_element_type.31
  649.2 94.3 %reduce-scatter.6.cloned.1.call-done = f32[512,128]{1,0:T(8,128)} async-done(((f32[512,1024]{1,0:T(8,128)}), f32[512,128]{1,0:T(8,128)}) %reduce-scatter.6.cloned.1.call-update) | async-done | bytes 262160 | tf_op jit(solution)/shard_map/reduce_scatter | solution.py:111
  743.5 1.6 convert_element_type.30
  745.1 149.0 %reduce-scatter.4.cloned.1.call-done = f32[8,5120]{1,0:T(8,128)} async-done(((f32[256,5120]{1,0:T(8,128)}), f32[8,5120]{1,0:T(8,128)}) %reduce-scatter.4.cloned.1.call-update) | async-done | bytes 163856 | tf_op jit(solution)/shard_map/reduce_scatter | solution.py:108
  894.1 1.6 convert_element_type.29
  (269 shorter events, 111.6 us)
Async XLA Ops:
  7.2 67.8 %all-gather.7.cloned.1.call-start = ((), (), s32[]{:S(2)}) async-start(), calls=%async_computation.3 | async-start | bytes 2703360 | tf_op jit(solution)/shard_map/all_gather | solution.py:30
  7.9 130.0 %all-gather.9.cloned.1.call-start = ((), (), s32[]{:S(2)}) async-start(), calls=%async_computation.4 | async-start | bytes 2703360 | tf_op jit(solution)/shard_map/all_gather | solution.py:31
  8.6 189.1 %all-gather.11.cloned.1.call-start = ((), (), s32[]{:S(2)}) async-start(), calls=%async_computation.8 | async-start | bytes 1351680 | tf_op jit(solution)/shard_map/all_gather | solution.py:14
  79.4 58.4 %copy-start.2 = (s32[1,2]{1,0:T(1,128)S(1)}, s32[1,2]{1,0:T(1,128)}, u32[]{:S(2)}) copy-start(s32[1,2]{1,0:T(1,128)} %param.19) | copy-start | bytes 28
  136.5 0.6 copy-start.1
  137.1 121.2 %all-gather.13.cloned.1.call-start = ((), (), s32[]{:S(2)}) async-start(), calls=%async_computation.9 | async-start | bytes 1351680 | tf_op jit(solution)/shard_map/all_gather | solution.py:14
  137.7 509.9 %reduce-scatter.8.cloned.1.call-start = ((), (), s32[]{:S(2)}) async-start(), calls=%async_computation.7 | async-start | bytes 2359296 | tf_op jit(solution)/shard_map/reduce_scatter | solution.py:112
  258.4 2.3 copy-start
  550.3 193.3 %reduce-scatter.6.cloned.1.call-start = ((), (), s32[]{:S(2)}) async-start(), calls=%async_computation.6 | async-start | bytes 2359296 | tf_op jit(solution)/shard_map/reduce_scatter | solution.py:111
  550.8 343.3 %reduce-scatter.4.cloned.1.call-start = ((), (), s32[]{:S(2)}) async-start(), calls=%async_computation.5 | async-start | bytes 5406720 | tf_op jit(solution)/shard_map/reduce_scatter | solution.py:108
Sparse Core Ops, SparseCore 0:
  9.9 65.0 all-gather.6
  76.8 60.0 all-gather.8
  139.3 58.3 all-gather.10
  200.0 58.2 all-gather.12
  550.4 97.1 reduce-scatter.7
  652.1 91.3 reduce-scatter.5
  746.1 147.9 reduce-scatter.3
where the time goes:
time: 909 us; the launch traced here: 903 us
  waiting for transfers between devices  524 us (58%)
  blocking collectives  130 us (14%)
  matrix products  91.9 us (10%)
  local copies, waits for them, and re-layouts  74.2 us (8%)
  loops' own time  38.4 us (4%)
  other arithmetic  29.7 us (3%)
  between operations  14.2 us (2%)
    reduce_scatter x1, waiting for transfers between devices, on_device(): lax.psum_scatter(dq_term, 'ctx', scatter_dimension=0, tiled=True)  149 us
    psum x1, blocking collectives, on_device(): row_dot = lax.psum(lax.map(local_dot, heads), 'ctx')  130 us
    all_gather x2, waiting for transfers between devices, merged(): pieces = jax.tree.map(lambda part: lax.all_gather(part, axis), value)  115 us
    reduce_scatter x1, waiting for transfers between devices, on_device(): lax.psum_scatter(dv_term, 'group', scatter_dimension=1, tiled=True)  96 us
    reduce_scatter x1, waiting for transfers between devices, on_device(): lax.psum_scatter(dk_term, 'group', scatter_dimension=1, tiled=True)  94.3 us
    all_gather x1, waiting for transfers between devices, on_device(): lax.all_gather(queries, 'ctx', axis=0, tiled=True)  66.3 us
    dot_general x24, matrix products, scores_of(): jnp.einsum('rgd,kd->grk', q_head, k_head, preferred_element_type=jnp.floa...  39.6 us
    another operation x1, loops' own time, on_device(): row_dot = lax.psum(lax.map(local_dot, heads), 'ctx')  26.4 us
  transfers between devices with their start and end apart: 7, of which 6 were waited for; matrix products, arithmetic and copies ran while one was open for 7% of the time, Pallas kernels for 0%

commit v1 on v0

v1 whole, which is shorter than its diff:
```python
import functools
import math

import jax
import jax.numpy as jnp
from jax import lax
from jax.experimental import pallas as pl
from jax.experimental.pallas import tpu as pltpu
from jax.sharding import PartitionSpec as P

QH = 40
KH = 8
HD = 128
SHARE = QH // KH
WINDOW = 128
SPAN = 512
OWN = 8
BLK = OWN * SHARE
UNIT = 16 * BLK
KT = 256
KEYS = 4 * SPAN
NT = KEYS // KT
SCALE = 1.0 / math.sqrt(HD)
LOG2 = SCALE * math.log2(math.e)
TRANS = (((1,), (1,)), ((), ()))
MESH = pl.DeviceIdType.MESH
F32 = jnp.float32
BF16 = jnp.bfloat16


def dot(a, b):
    return jnp.dot(a, b, preferred_element_type=F32)


def dot_t(a, b):
    return lax.dot_general(a, b, TRANS, preferred_element_type=F32)


def wide(rows):
    return jnp.concatenate([rows[i : i + 1] for i in range(SHARE)], axis=1)


def tall(row):
    return jnp.concatenate([row[:, i * HD : (i + 1) * HD] for i in range(SHARE)], axis=0)


def kernel(
    plen_ref, rlen_ref, q_ref, do_ref, k_hbm, v_hbm,
    dq_ref, dk_ref, dv_ref,
    snd, gath, q_s, do_s, kv, k_t, e_buf, dp_buf, mst, st_all, dka, dva,
    dq_own, dq_out, dq_in, z_out, z_in, f_out, f_in, c_out, c_in, zz_out, zz_in,
    loc_sem, kv_send, kv_recv, s1_send, s1_recv, x_send, x_recv, st_send, st_recv,
    dq_send, dq_recv, z_sem, f_send, f_recv, c_sem, zz_sem,
):
    g = lax.axis_index("group")
    c = lax.axis_index("ctx")
    core = c % 2
    z_lo = (c // 2) % 4
    x = c // 8
    par = z_lo % 2
    zl = z_lo // 2
    me16 = zl * 8 + g
    me8 = x * 2 + zl
    other = 1 - zl

    def ctx_of(x_, z_lo_, core_):
        return (x_ * 4 + z_lo_) * 2 + core_

    sib = (g, ctx_of(x, z_lo, 1 - core))
    zp_lo = z_lo + 1 - 2 * par
    zp = (g, ctx_of(x, zp_lo, core))
    mate = (g, ctx_of(x, other * 2 + par, core))

    def plane(k):
        dest = (me16 + k) % 16
        return (dest % 8, ctx_of(x, (dest // 8) * 2 + par, core))

    def ring(k):
        dest = (me8 + k) % 8
        return (g, ctx_of(dest // 2, (dest % 2) * 2 + par, core))

    def at_x(k):
        return (g, ctx_of((x + k) % 4, z_lo, core))

    def remote(src, dst, send, recv, dev):
        return pltpu.make_async_remote_copy(
            src_ref=src, dst_ref=dst, send_sem=send, recv_sem=recv, device_id=dev, device_id_type=MESH
        )

    barrier = pltpu.get_barrier_semaphore()

    def greet(dev):
        pl.semaphore_signal(barrier, inc=1, device_id=dev, device_id_type=MESH)

    lax.fori_loop(1, 16, lambda k, s: (greet(plane(k)), s)[1], 0)
    for dx in (1, 2, 3):
        for z_ in (zl, other):
            greet((g, ctx_of((x + dx) % 4, z_ * 2 + par, core)))
    greet(sib)
    greet(zp)

    cols = pl.ds(pl.multiple_of(g * HD, HD), HD)
    local = [
        pltpu.make_async_copy(h.at[:, cols], kv.at[0, i], loc_sem.at[i]) for i, h in enumerate((k_hbm, v_hbm))
    ]
    for cp in local:
        cp.start()

    qf = q_ref[...].astype(F32)
    live_to = rlen_ref[0, c // 16]
    t_row = (c % 16) * OWN + lax.broadcasted_iota(jnp.int32, (OWN, 1), 0)
    dof = jnp.where(t_row < live_to, do_ref[...].astype(F32), 0.0)
    for b in range(KH):
        rows = [m[:, (b * SHARE + a) * HD : (b * SHARE + a + 1) * HD] for m in (qf, dof) for a in range(SHARE)]
        snd[b] = jnp.concatenate(rows, axis=0).astype(BF16)
    gath[x, me16] = snd[g]

    pl.semaphore_wait(barrier, 23)

    def s1(k):
        return remote(snd.at[plane(k)[0]], gath.at[x, me16], s1_send.at[k], s1_recv.at[me16], plane(k))

    def s1_start(k, s):
        s1(k).start()
        return s

    lax.fori_loop(1, 16, s1_start, 0)

    def kv_copy(i, src, slot, dev):
        return remote(src, kv.at[slot, i], kv_send.at[slot, i], kv_recv.at[slot, i], dev)

    for i, h in enumerate((k_hbm, v_hbm)):
        kv_copy(i, h.at[:, cols], 2, zp).start()
        kv_copy(i, h.at[:, cols], 1, sib).start()

    dka[...] = jnp.zeros_like(dka)
    dva[...] = jnp.zeros_like(dva)

    plen = plen_ref[0]
    c_slots = [c, sib[1], zp[1], ctx_of(x, zp_lo, 1 - core)]

    def piece(x_, p):
        return gath.at[x_, pl.ds(p * 4, 4)]

    def x_copy(way, p):
        if way == 0:
            return remote(piece(x, p), piece(x, p), x_send.at[0, p], x_recv.at[0, p], at_x(1))
        if way == 1:
            return remote(piece(x, p), piece(x, p), x_send.at[1, p], x_recv.at[1, p], at_x(3))
        src = (x + 3) % 4 if p < 2 else (x + 1) % 4
        return remote(piece(src, p), piece(src, p), x_send.at[2, p], x_recv.at[2, p], at_x(1 if p < 2 else 3))

    def s1_wait(k, s):
        src = (me16 + k) % 16
        remote(snd.at[0], gath.at[x, src], s1_send.at[k], s1_recv.at[src], plane(k)).wait_recv()
        return s

    def st_copy(unit, k):
        return remote(
            st_all.at[unit, me8], st_all.at[unit, me8], st_send.at[unit, k], st_recv.at[unit, me8], ring(k)
        )

    def phase1(i, carry):
        unit = (x + i + i // 2 - 2 * (i // 3)) % 4

        @pl.when(i == 0)
        def _():
            lax.fori_loop(1, 16, s1_wait, 0)
            for p, r in ((0, 2), (1, 3), (2, 0), (3, 1)):
                x_copy(0, p).start()
                x_copy(1, r).start()
            for i_ in range(2):
                kv_copy(i_, kv.at[2, i_], 2, zp).wait_recv()
                kv_copy(i_, kv.at[2, i_], 3, sib).start()
            for cp in local:
                cp.wait()
            for i_ in range(2):
                kv_copy(i_, kv.at[1, i_], 1, sib).wait_recv()
            for i_ in range(2):
                kv_copy(i_, kv.at[3, i_], 3, sib).wait_recv()
            for slot in range(4):
                k_t[:, slot * SPAN : (slot + 1) * SPAN] = kv[slot, 0].astype(F32).T.astype(BF16)

        @pl.when(i == 1)
        def _():
            for p, r in ((0, 2), (1, 3)):
                x_copy(0, p).wait_recv()
                x_copy(2, p).start()
                x_copy(1, r).wait_recv()
                x_copy(2, r).start()
            for r in (0, 1):
                x_copy(1, r).wait_recv()

        @pl.when(i == 2)
        def _():
            for p in (2, 3):
                x_copy(0, p).wait_recv()

        @pl.when(i == 3)
        def _():
            for p in range(4):
                x_copy(2, p).wait_recv()

        both = gath[unit].astype(F32)
        qu = both[:, :BLK].reshape(UNIT, HD).astype(BF16)
        dou = both[:, BLK:].reshape(UNIT, HD).astype(BF16)
        q_s[unit] = qu
        do_s[unit] = dou
        tops, sums, dots = [], [], []
        for t in range(NT):
            slot, part = t * KT // SPAN, pl.ds(t * KT % SPAN, KT)
            rows = pl.ds(t * KT, KT)
            s = dot_t(kv[slot, 0, part], qu)
            if t % 2 == 1:
                place = c_slots[slot] * SPAN + KT + lax.broadcasted_iota(jnp.int32, (KT, 1), 0)
                s = jnp.where(place < plen, s, -1e30)
            dp = dot_t(kv[slot, 1, part], dou)
            top = jnp.max(s, axis=0, keepdims=True)
            e = jnp.exp2((s - top) * LOG2)
            e_buf[unit, rows] = e
            dp_buf[unit, rows] = dp
            tops.append(top)
            sums.append(jnp.sum(e, axis=0, keepdims=True))
            dots.append(jnp.sum(e * dp, axis=0, keepdims=True))
        top = functools.reduce(jnp.maximum, tops)
        total, rdot = 0.0, 0.0
        for t in range(NT):
            w = jnp.exp2((tops[t] - top) * LOG2)
            total = total + sums[t] * w
            rdot = rdot + dots[t] * w
        mst[unit] = jnp.concatenate(tops, axis=0)
        st_all[unit, me8] = jnp.concatenate([tall(top), tall(total), tall(rdot), jnp.zeros((1, HD), F32)], axis=0)

        def send(k, s):
            st_copy(unit, k).start()
            return s

        lax.fori_loop(1, 8, send, 0)
        return carry

    lax.fori_loop(0, 4, phase1, 0)

    def dq_copy(unit):
        return remote(dq_out.at[unit], dq_in.at[x], dq_send.at[unit], dq_recv.at[x], (g, ctx_of(unit, z_lo, core)))

    def phase2(i, carry):
        unit = (x + i) % 4

        def arrived(k, s):
            src = (me8 + k) % 8
            remote(
                st_all.at[unit, src], st_all.at[unit, src], st_send.at[unit, k], st_recv.at[unit, src], ring(k)
            ).wait_recv()
            return s

        lax.fori_loop(1, 8, arrived, 0)
        stats = st_all[unit]
        top = jnp.max(stats[:, 0:SHARE], axis=0)
        w = jnp.exp2((stats[:, 0:SHARE] - top[None]) * LOG2)
        total = jnp.sum(stats[:, SHARE : 2 * SHARE] * w, axis=0)
        rdot = jnp.sum(stats[:, 2 * SHARE : 3 * SHARE] * w, axis=0) / total
        top, inv, rdot = wide(top), wide(1.0 / total), wide(rdot)
        qu, dou = q_s[unit], do_s[unit]
        factor = jnp.exp2((mst[unit] - top) * LOG2) * inv
        dq_t = jnp.zeros((HD, UNIT), F32)
        for t in range(NT):
            rows = pl.ds(t * KT, KT)
            p = e_buf[unit, rows] * factor[t : t + 1]
            ds = (p * (dp_buf[unit, rows] - rdot)).astype(BF16)
            dva[rows] += dot(p.astype(BF16), dou)
            dka[rows] += dot(ds, qu)
            dq_t += dot(k_t[:, rows], ds)
        dq = dq_t.T * SCALE

        @pl.when(i < 4)
        def _():
            dq_out[unit] = dq.astype(BF16)
            dq_copy(unit).start()

        @pl.when(i == 4)
        def _():
            dq_own[...] = dq

        return carry

    lax.fori_loop(1, 5, phase2, 0)

    for n, slot in enumerate((1, 3)):
        rows = pl.ds(slot * SPAN, SPAN)
        c_out[n, 0] = (dka[rows] * SCALE).astype(BF16)
        c_out[n, 1] = dva[rows].astype(BF16)
    c_copy = remote(c_out, c_in, c_sem.at[0], c_sem.at[1], sib)
    c_copy.start()

    tot = dq_own[...]
    for k in (1, 2, 3):
        src = (x + k) % 4
        remote(dq_out.at[src], dq_in.at[src], dq_send.at[src], dq_recv.at[src], at_x(k)).wait_recv()
        tot = tot + dq_in[src].astype(F32)
    dq_own[...] = tot
    z_out[...] = dq_own[pl.ds(pl.multiple_of(other * 320, 320), 320)].astype(BF16)
    z_copy = remote(z_out, z_in, z_sem.at[0], z_sem.at[1], mate)
    z_copy.start()

    c_copy.wait_recv()
    far = pl.ds(2 * SPAN, SPAN)
    zz_out[0] = (dka[far] * SCALE + c_in[1, 0].astype(F32)).astype(BF16)
    zz_out[1] = (dva[far] + c_in[1, 1].astype(F32)).astype(BF16)
    zz_copy = remote(zz_out, zz_in, zz_sem.at[0], zz_sem.at[1], zp)
    zz_copy.start()

    z_copy.wait_recv()
    mine = dq_own[pl.ds(pl.multiple_of(zl * 320, 320), 320)] + z_in[...].astype(F32)
    for b in range(8):
        f_out[b] = jnp.concatenate([mine[b * BLK : (b + 1) * BLK], jnp.zeros((8, HD), F32)], axis=0).astype(BF16)
    f_in[g] = f_out[g]

    def f_copy(k):
        dest = (g + k) % 8
        return remote(f_out.at[dest], f_in.at[g], f_send.at[k], f_recv.at[g], (dest, c))

    def f_start(k, s):
        f_copy(k).start()
        return s

    lax.fori_loop(1, 8, f_start, 0)

    zz_copy.wait_recv()
    near = pl.ds(0, SPAN)
    dk_ref[...] = (dka[near] * SCALE + c_in[0, 0].astype(F32) + zz_in[0].astype(F32)).astype(BF16)
    dv_ref[...] = (dva[near] + c_in[0, 1].astype(F32) + zz_in[1].astype(F32)).astype(BF16)

    def f_wait(k, s):
        src = (g + k) % 8
        remote(f_out.at[src], f_in.at[src], f_send.at[k], f_recv.at[src], (src, c)).wait_recv()
        return s

    lax.fori_loop(1, 8, f_wait, 0)
    out = []
    for b in range(8):
        blk = f_in[b].astype(F32)
        out += [blk[a * OWN : (a + 1) * OWN] for a in range(SHARE)]
    dq_ref[...] = jnp.concatenate(out, axis=1).astype(BF16)

    def drain1(k, s):
        s1(k).wait_send()
        return s

    lax.fori_loop(1, 16, drain1, 0)
    for i in range(2):
        kv_copy(i, kv.at[2, i], 2, zp).wait_send()
        kv_copy(i, kv.at[1, i], 1, sib).wait_send()
        kv_copy(i, kv.at[3, i], 3, sib).wait_send()
    for way in range(3):
        for p in range(4):
            x_copy(way, p).wait_send()

    def drain_st(n, s):
        st_copy(n // 7, n % 7 + 1).wait_send()
        return s

    lax.fori_loop(0, 28, drain_st, 0)
    for k in (1, 2, 3):
        dq_copy((x + k) % 4).wait_send()

    def drain_f(k, s):
        f_copy(k).wait_send()
        return s

    lax.fori_loop(1, 8, drain_f, 0)
    c_copy.wait_send()
    z_copy.wait_send()
    zz_copy.wait_send()


def on_device(queries, grad_out, keys, values, prompt_len, resp_len):
    vmem = pl.BlockSpec(memory_space=pltpu.VMEM)
    smem = pl.BlockSpec(memory_space=pltpu.SMEM)
    hbm = pl.BlockSpec(memory_space=pl.ANY)
    dma = pltpu.SemaphoreType.DMA
    return pl.pallas_call(
        kernel,
        out_shape=[
            jax.ShapeDtypeStruct((OWN, QH * HD), BF16),
            jax.ShapeDtypeStruct((SPAN, HD), BF16),
            jax.ShapeDtypeStruct((SPAN, HD), BF16),
        ],
        in_specs=[smem, smem, vmem, vmem, hbm, hbm],
        out_specs=[vmem, vmem, vmem],
        scratch_shapes=[
            pltpu.VMEM((KH, 2 * BLK, HD), BF16),
            pltpu.VMEM((4, 16, 2 * BLK, HD), BF16),
            pltpu.VMEM((4, UNIT, HD), BF16),
            pltpu.VMEM((4, UNIT, HD), BF16),
            pltpu.VMEM((4, 2, SPAN, HD), BF16),
            pltpu.VMEM((HD, KEYS), BF16),
            pltpu.VMEM((4, KEYS, UNIT), F32),
            pltpu.VMEM((4, KEYS, UNIT), F32),
            pltpu.VMEM((4, NT, UNIT), F32),
            pltpu.VMEM((4, 8, 16, HD), F32),
            pltpu.VMEM((KEYS, HD), F32),
            pltpu.VMEM((KEYS, HD), F32),
            pltpu.VMEM((UNIT, HD), F32),
            pltpu.VMEM((4, UNIT, HD), BF16),
            pltpu.VMEM((4, UNIT, HD), BF16),
            pltpu.VMEM((UNIT // 2, HD), BF16),
            pltpu.VMEM((UNIT // 2, HD), BF16),
            pltpu.VMEM((8, BLK + 8, HD), BF16),
            pltpu.VMEM((8, BLK + 8, HD), BF16),
            pltpu.VMEM((2, 2, SPAN, HD), BF16),
            pltpu.VMEM((2, 2, SPAN, HD), BF16),
            pltpu.VMEM((2, SPAN, HD), BF16),
            pltpu.VMEM((2, SPAN, HD), BF16),
            dma((2,)),
            dma((4, 2)),
            dma((4, 2)),
            dma((16,)),
            dma((16,)),
            dma((3, 4)),
            dma((3, 4)),
            dma((4, 8)),
            dma((4, 8)),
            dma((4,)),
            dma((4,)),
            dma((2,)),
            dma((8,)),
            dma((8,)),
            dma((2,)),
            dma((2,)),
        ],
        compiler_params=pltpu.CompilerParams(
            collective_id=0, has_side_effects=True, vmem_limit_bytes=60 * 2**20
        ),
        name="window_grads",
    )(prompt_len, resp_len, queries, grad_out, keys, values)


def solution(mesh):
    in_specs = (
        P(("group", "ctx"), None),
        P(("group", "ctx"), None),
        P("ctx", None),
        P("ctx", None),
        P(),
        P("group", None),
    )
    out_specs = (P(("group", "ctx"), None), P("ctx", "group"), P("ctx", "group"))
    return jax.shard_map(
        on_device, mesh=mesh, in_specs=in_specs, out_specs=out_specs, check_vma=False
    )
```

time: 909 us -> 74.5 us (0.08)
  the two profiles are of different devices: /device:TPU:1 before, /device:TPU:38 now
where the time goes in v1:
time: 74.5 us; the launch traced here: 74.3 us
  Pallas kernels  69.9 us (94%)
  local copies, waits for them, and re-layouts  3.17 us (4%)
  between operations  1.3 us (2%)
    pallas_call x1, Pallas kernels, on_device(): pl.pallas_call(kernel, out_shape=[jax.ShapeDtypeStruct((OWN, QH * HD), BF...  69.9 us
    unnamed x7, local copies, waits for them, and re-layouts  3.17 us

profile of v1, /device:TPU:38, one launch (start us, length us, event | category | flops | bytes accessed | tf_op | source)
XLA Modules:
  0.0 74.3 jit_solution(17256403862003676263)
XLA Ops:
  1.3 69.9 %window_grads.1 = (bf16[8,5120]{1,0:T(8,128)(2,1)}, bf16[512,128]{1,0:T(8,128)(2,1)}, bf16[512,128]{1,0:T(8,128)(2,1)}) custom-call(s32[1]{0:T(128)S(6)} %copy.12.plen_ref, s32[1,2]{1,0:T(1,128)} %rlen_ref.1, bf16[8,5120]{1,0:T(8,128)(2,1)} %q_ref.1, bf16[8,5120]{1,0:T(8,128)(2,1)} %do_ref.1, bf16[512,1024]{1,0:T(8,128)(2,1)} %k_hbm.1, bf16[512,1024]{1,0:T(8,128)(2,1)} %v_hbm.1), custom_call_target="tpu_custom_call" | custom-call | tf_op jit(solution)/shard_map/window_grads/pallas_call | solution.py:381
  71.1 0.0 copy-start.1
  71.2 1.6 %copy.13 = bf16[8,5120]{1,0:T(8,128)(2,1)} copy(bf16[8,5120]{1,0:T(8,128)(2,1)} %get-tuple-element.6) | data formatting | bytes 163840
  72.7 0.0 copy-done.1
  72.7 0.0 copy-start
  72.7 0.7 copy.14
  73.4 0.3 copy-done
  73.7 0.7 copy.15
Async XLA Ops:
  71.1 1.6 %copy-start.1 = (bf16[512,128]{1,0:T(8,128)(2,1)S(1)}, bf16[512,128]{1,0:T(8,128)(2,1)}, u32[]{:S(2)}) copy-start(bf16[512,128]{1,0:T(8,128)(2,1)} %get-tuple-element.7) | copy-start | bytes 393220
  72.7 1.0 %copy-start = (bf16[512,128]{1,0:T(8,128)(2,1)S(1)}, bf16[512,128]{1,0:T(8,128)(2,1)}, u32[]{:S(2)}) copy-start(bf16[512,128]{1,0:T(8,128)(2,1)} %get-tuple-element.8) | copy-start | bytes 393220

commit v2 on v1

v2 whole, which is shorter than its diff:
```python
import functools
import math

import jax
import jax.numpy as jnp
from jax import lax
from jax.experimental import pallas as pl
from jax.experimental.pallas import tpu as pltpu
from jax.sharding import PartitionSpec as P

QH = 40
KH = 8
HD = 128
SHARE = QH // KH
WINDOW = 128
SPAN = 512
OWN = 8
BLK = OWN * SHARE
UNIT = 16 * BLK
KT = 256
KEYS = 4 * SPAN
NT = KEYS // KT
SCALE = 1.0 / math.sqrt(HD)
LOG2 = SCALE * math.log2(math.e)
TRANS = (((1,), (1,)), ((), ()))
MESH = pl.DeviceIdType.MESH
F32 = jnp.float32
BF16 = jnp.bfloat16


def dot(a, b):
    return jnp.dot(a, b, preferred_element_type=F32)


def dot_t(a, b):
    return lax.dot_general(a, b, TRANS, preferred_element_type=F32)


def wide(rows):
    return jnp.concatenate([rows[i : i + 1] for i in range(SHARE)], axis=1)


def tall(row):
    return jnp.concatenate([row[:, i * HD : (i + 1) * HD] for i in range(SHARE)], axis=0)


def kernel(
    plen_ref, rlen_ref, q_ref, do_ref, k_hbm, v_hbm,
    dq_ref, dk_ref, dv_ref,
    snd, held, gath, q_s, do_s, kv, k_t, e_buf, dp_buf, mst, st_loc, st_all, rdots, dka, dva, dq_acc,
    r_out, r_in, f_out, f_in, c_out, c_in, zz_out, zz_in,
    loc_sem, kv_send, kv_recv, z_send, z_recv, g_send, g_recv, st_send, st_recv,
    r_send, r_recv, f_send, f_recv, c_sem, zz_sem,
):
    g = lax.axis_index("group")
    c = lax.axis_index("ctx")
    core = c % 2
    z_lo = (c // 2) % 4
    x = c // 8
    par = z_lo % 2
    zl = z_lo // 2
    y = g // 2
    z_hi = g % 2
    zq = z_hi * 2 + zl
    pq = z_hi * 2 + 1 - zl
    order = [zq, pq, 3 - zq, 3 - pq]
    me16 = zq * 4 + y
    me8 = x * 2 + zl

    def ctx_of(x_, z_lo_, core_):
        return (x_ * 4 + z_lo_) * 2 + core_

    sib = (g, ctx_of(x, z_lo, 1 - core))
    zp_lo = z_lo + 1 - 2 * par
    zp = (g, ctx_of(x, zp_lo, core))
    mate = (g, ctx_of(x, (1 - zl) * 2 + par, core))

    def place(dest):
        z_ = dest // 4
        return ((dest % 4) * 2 + z_ // 2, ctx_of(x, (z_ % 2) * 2 + par, core))

    def ring(k):
        dest = (me8 + k) % 8
        return (g, ctx_of(dest // 2, (dest % 2) * 2 + par, core))

    def at_x(k):
        return (g, ctx_of((x + k) % 4, z_lo, core))

    def remote(src, dst, send, recv, dev):
        return pltpu.make_async_remote_copy(
            src_ref=src, dst_ref=dst, send_sem=send, recv_sem=recv, device_id=dev, device_id_type=MESH
        )

    def repeat(first, last, step):
        def body(k, s):
            step(k)
            return s

        lax.fori_loop(first, last, body, 0)

    def level(k):
        return (((y + k) % 4) * 2 + z_hi, ctx_of((x + k // 4) % 4, z_lo, core))

    barrier = pltpu.get_barrier_semaphore()

    def greet(dev):
        pl.semaphore_signal(barrier, inc=1, device_id=dev, device_id_type=MESH)

    repeat(1, 16, lambda k: greet(level(k)))
    repeat(0, 12, lambda k: greet(place((zq * 4 + 4 + k) % 16)))
    for dx in (1, 2, 3):
        greet((g, ctx_of((x + dx) % 4, (1 - zl) * 2 + par, core)))
    greet(sib)
    greet(zp)

    cols = pl.ds(pl.multiple_of(g * HD, HD), HD)
    local = [
        pltpu.make_async_copy(h.at[:, cols], kv.at[0, i], loc_sem.at[i]) for i, h in enumerate((k_hbm, v_hbm))
    ]
    for cp in local:
        cp.start()

    qf = q_ref[...].astype(F32)
    live_to = rlen_ref[0, c // 16]
    t_row = (c % 16) * OWN + lax.broadcasted_iota(jnp.int32, (OWN, 1), 0)
    dof = jnp.where(t_row < live_to, do_ref[...].astype(F32), 0.0)
    for b in range(KH):
        rows = [m[:, (b * SHARE + a) * HD : (b * SHARE + a + 1) * HD] for m in (qf, dof) for a in range(SHARE)]
        snd[b % 2, b // 2] = jnp.concatenate(rows, axis=0).astype(BF16)
    gath[zq, x * 4 + y] = snd[z_hi, y]

    pl.semaphore_wait(barrier, 32)

    def z_copy(r):
        dest = order[r]
        half = z_hi if r == 1 else 1 - z_hi
        return remote(snd.at[half], held.at[zq], z_send.at[r], z_recv.at[r], place(dest * 4 + y))

    def g_copy(r, k):
        zr = order[r]
        head = (y + k) % 4
        src = snd.at[z_hi, head] if r == 0 else held.at[zr, head]
        return remote(src, gath.at[zr, x * 4 + y], g_send.at[r], g_recv.at[r], level(k))

    def spread(r):
        if r > 0:
            z_copy(r).wait_recv()
            gath[order[r], x * 4 + y] = held[order[r], y]
        repeat(1, 16, lambda k: g_copy(r, k).start())

    def all15(r):
        part = gath.at[order[r], pl.ds(0, 15)]
        return remote(part, part, g_send.at[r], g_recv.at[r], level(1))

    z_copy(1).start()
    z_copy(2).start()
    spread(0)
    z_copy(3).start()

    def kv_copy(i, src, slot, dev):
        return remote(src, kv.at[slot, i], kv_send.at[slot, i], kv_recv.at[slot, i], dev)

    for i, h in enumerate((k_hbm, v_hbm)):
        kv_copy(i, h.at[:, cols], 1, sib).start()

    dka[...] = jnp.zeros_like(dka)
    dva[...] = jnp.zeros_like(dva)
    dq_acc[...] = jnp.zeros_like(dq_acc)
    st_loc[...] = jnp.concatenate([jnp.full((4, 1, UNIT), -1e30, F32), jnp.zeros((4, 7, UNIT), F32)], axis=1)

    spread(1)
    for i, h in enumerate((k_hbm, v_hbm)):
        kv_copy(i, h.at[:, cols], 2, zp).start()
    spread(2)
    for cp in local:
        cp.wait()
    for i in range(2):
        kv_copy(i, kv.at[1, i], 1, sib).wait_recv()

    plen = plen_ref[0]
    c_zp = zp[1]
    c_base = [c * SPAN, sib[1] * SPAN, c_zp * SPAN, (c_zp + 1 - 2 * core) * SPAN]

    def st_copy(unit, k):
        return remote(
            st_all.at[unit, me8], st_all.at[unit, me8], st_send.at[unit], st_recv.at[unit], ring(k)
        )

    def st_seven(unit):
        part = st_all.at[unit, pl.ds(0, 7)]
        return remote(part, part, st_send.at[unit], st_recv.at[unit], ring(1))

    def source(r):
        same = (1 - r // 2) * z_hi + (r // 2) * (1 - z_hi)
        mine = (1 - r % 2) * zl + (r % 2) * (1 - zl)
        return same * 2 + (1 - r // 2) * mine + (r // 2) * (1 - mine)

    def phase1(i, carry):
        unit = source(jnp.where(i < 6, i % 3, 3))
        half = jnp.where(i < 6, i // 3, i - 6)

        @pl.when(i == 0)
        def _():
            all15(0).wait_recv()

        @pl.when(i == 1)
        def _():
            spread(3)
            all15(1).wait_recv()

        @pl.when(i == 2)
        def _():
            for i_ in range(2):
                kv_copy(i_, kv.at[2, i_], 2, zp).wait_recv()
                kv_copy(i_, kv.at[2, i_], 3, sib).start()
            all15(2).wait_recv()

        @pl.when(i == 3)
        def _():
            for i_ in range(2):
                kv_copy(i_, kv.at[3, i_], 3, sib).wait_recv()

        @pl.when(i == 6)
        def _():
            all15(3).wait_recv()

        @pl.when(half == 0)
        def _():
            both = gath[unit].astype(F32)
            q_s[unit] = both[:, :BLK].reshape(UNIT, HD).astype(BF16)
            do_s[unit] = both[:, BLK:].reshape(UNIT, HD).astype(BF16)

        def cell():
            qu, dou = q_s[unit], do_s[unit]
            old = st_loc[unit]
            tops, sums, dots = [old[0:1]], [old[1:2]], [old[2:3]]
            for t in range(NT // 2):
                slot, part = half * 2 + t // 2, pl.ds(t % 2 * KT, KT)
                rows = pl.ds(pl.multiple_of(half * 2 * SPAN + t * KT, KT), KT)
                s = dot_t(kv[slot, 0, part], qu)
                if t % 2 == 1:
                    base = jnp.where(half == 0, c_base[t // 2], c_base[2 + t // 2]) + KT
                    at = base + lax.broadcasted_iota(jnp.int32, (KT, 1), 0)
                    s = jnp.where(at < plen, s, -1e30)
                dp = dot_t(kv[slot, 1, part], dou)
                top = jnp.max(s, axis=0, keepdims=True)
                e = jnp.exp2((s - top) * LOG2)
                e_buf[unit, rows] = e
                dp_buf[unit, rows] = dp
                tops.append(top)
                sums.append(jnp.sum(e, axis=0, keepdims=True))
                dots.append(jnp.sum(e * dp, axis=0, keepdims=True))
            top = functools.reduce(jnp.maximum, tops)
            total, rdot = 0.0, 0.0
            for t in range(NT // 2 + 1):
                w = jnp.exp2((tops[t] - top) * LOG2)
                total = total + sums[t] * w
                rdot = rdot + dots[t] * w
            mst[unit, half] = jnp.concatenate(tops[1:], axis=0)
            st_loc[unit, 0:3] = jnp.concatenate([top, total, rdot], axis=0)

        cell()

        @pl.when(half == 1)
        def _():
            s = st_loc[unit]
            st_all[unit, me8] = jnp.concatenate([tall(s[0:1]), tall(s[1:2]), tall(s[2:3]), jnp.zeros((1, HD), F32)], axis=0)
            repeat(1, 8, lambda k: st_copy(unit, k).start())

        return carry

    def drain_a():
        for r in range(4):
            all15(r).wait_send()
        for r in (1, 2, 3):
            z_copy(r).wait_send()
        for i in range(2):
            kv_copy(i, kv.at[2, i], 2, zp).wait_send()
            kv_copy(i, kv.at[1, i], 1, sib).wait_send()
            kv_copy(i, kv.at[3, i], 3, sib).wait_send()
        repeat(0, 4, lambda u: st_seven(u).wait_send())

    lax.fori_loop(0, 8, phase1, 0)

    for slot in range(4):
        k_t[slot // 2, :, slot % 2 * SPAN : (slot % 2 + 1) * SPAN] = kv[slot, 0].astype(F32).T.astype(BF16)

    def combine(unit):
        st_seven(unit).wait_recv()
        stats = st_all[unit]
        top = jnp.max(stats[:, 0:SHARE], axis=0)
        w = jnp.exp2((stats[:, 0:SHARE] - top[None]) * LOG2)
        total = jnp.sum(stats[:, SHARE : 2 * SHARE] * w, axis=0)
        rdot = jnp.sum(stats[:, 2 * SHARE : 3 * SHARE] * w, axis=0) / total
        top, inv = wide(top), wide(1.0 / total)
        rdots[unit] = wide(rdot)
        mst[unit] = jnp.exp2((mst[unit] - top[None]) * LOG2) * inv[None]


    c_copy = [remote(c_out.at[n], c_in.at[n], c_sem.at[0, n], c_sem.at[1, n], sib) for n in range(2)]
    zz_copy = remote(zz_out, zz_in, zz_sem.at[0], zz_sem.at[1], zp)

    def r_copy(r, k):
        dest = (x + k) % 4
        return remote(r_out.at[r, dest], r_in.at[r, x], r_send.at[r], r_recv.at[r], at_x(k))

    def r_three(r):
        part = r_in.at[r, pl.ds(0, 3)]
        return remote(part, part, r_send.at[r], r_recv.at[r], at_x(1))

    def scatter(r):
        dq = dq_acc[order[r]]
        for n in range(4):
            r_out[r, n] = dq[n * 4 * BLK : (n + 1) * 4 * BLK].astype(BF16)
        for k in (1, 2, 3):
            r_copy(r, k).start()

    def f_copy(r, k):
        head = (y + k) % 4
        return remote(f_out.at[r, head], f_in.at[me16], f_send.at[r], f_recv.at[r], place(order[r] * 4 + head))

    def f_part(r):
        count = 3 if r == 0 else 4
        part = f_in.at[pl.ds(0, count)]
        return remote(part, part, f_send.at[r], f_recv.at[r], place(order[r] * 4 + y))

    def deliver(r):
        r_three(r).wait_recv()
        tot = dq_acc[order[r], pl.ds(pl.multiple_of(x * 4 * BLK, 4 * BLK), 4 * BLK)]
        for k in (1, 2, 3):
            tot = tot + r_in[r, (x + k) % 4].astype(F32)
        pad = jnp.zeros((8, HD), F32)
        for n in range(4):
            f_out[r, n] = jnp.concatenate([tot[n * BLK : (n + 1) * BLK], pad], axis=0).astype(BF16)
        if r == 0:
            f_in[me16] = f_out[0, y]
        repeat(1 if r == 0 else 0, 4, lambda k: f_copy(r, k).start())

    def c_start(n):
        rows = pl.ds((1 + 2 * n) * SPAN, SPAN)
        c_out[n, 0] = (dka[rows] * SCALE).astype(BF16)
        c_out[n, 1] = dva[rows].astype(BF16)
        c_copy[n].start()

    def phase2(i, carry):
        r = jnp.where(i < 3, 1 - i % 2, jnp.where(i < 7, 2 + (i // 4) * (1 - i // 6), 0))
        unit = source(r)
        half = jnp.where(i < 5, 1 - (i // 2) * (1 - i // 3), 0)

        @pl.when(i < 2)
        def _():
            combine(unit)

        @pl.when((i == 3) | (i == 4))
        def _():
            combine(unit)

        def cell():
            qu, dou = q_s[unit], do_s[unit]
            factor, rdot = mst[unit, half], rdots[unit]
            dq_t = jnp.zeros((HD, UNIT), F32)
            for t in range(NT // 2):
                rows = pl.ds(pl.multiple_of(half * 2 * SPAN + t * KT, KT), KT)
                p = e_buf[unit, rows] * factor[t : t + 1]
                ds = (p * (dp_buf[unit, rows] - rdot)).astype(BF16)
                dva[rows] += dot(p.astype(BF16), dou)
                dka[rows] += dot(ds, qu)
                dq_t += dot(k_t[half, :, t * KT : (t + 1) * KT], ds)
            dq_acc[unit] += dq_t.T * SCALE

        cell()

        @pl.when(i == 2)
        def _():
            scatter(1)

        @pl.when(i == 4)
        def _():
            c_start(1)

        @pl.when(i == 5)
        def _():
            scatter(3)
            c_copy[1].wait_recv()
            far = pl.ds(2 * SPAN, SPAN)
            zz_out[0] = (dka[far] * SCALE + c_in[1, 0].astype(F32)).astype(BF16)
            zz_out[1] = (dva[far] + c_in[1, 1].astype(F32)).astype(BF16)
            zz_copy.start()

        @pl.when(i == 6)
        def _():
            scatter(2)
            deliver(1)

        return carry

    lax.fori_loop(0, 8, phase2, 0)
    scatter(0)
    c_start(0)
    deliver(3)
    deliver(2)
    deliver(0)

    c_copy[0].wait_recv()
    near = pl.ds(0, SPAN)
    dka[near] = dka[near] * SCALE + c_in[0, 0].astype(F32)
    dva[near] = dva[near] + c_in[0, 1].astype(F32)
    zz_copy.wait_recv()
    dk_ref[...] = (dka[near] + zz_in[0].astype(F32)).astype(BF16)
    dv_ref[...] = (dva[near] + zz_in[1].astype(F32)).astype(BF16)

    for r in range(4):
        f_part(r).wait_recv()
    out = []
    for b in range(KH):
        first = (b % 2) * 8 + b // 2
        blk = f_in[first].astype(F32) + f_in[first + 4].astype(F32)
        out += [blk[a * OWN : (a + 1) * OWN] for a in range(SHARE)]
    dq_ref[...] = jnp.concatenate(out, axis=1).astype(BF16)

    drain_a()
    for n in range(2):
        c_copy[n].wait_send()
    zz_copy.wait_send()
    for r in range(4):
        r_three(r).wait_send()
        f_part(r).wait_send()


def on_device(queries, grad_out, keys, values, prompt_len, resp_len):
    vmem = pl.BlockSpec(memory_space=pltpu.VMEM)
    smem = pl.BlockSpec(memory_space=pltpu.SMEM)
    hbm = pl.BlockSpec(memory_space=pl.ANY)
    dma = pltpu.SemaphoreType.DMA
    return pl.pallas_call(
        kernel,
        out_shape=[
            jax.ShapeDtypeStruct((OWN, QH * HD), BF16),
            jax.ShapeDtypeStruct((SPAN, HD), BF16),
            jax.ShapeDtypeStruct((SPAN, HD), BF16),
        ],
        in_specs=[smem, smem, vmem, vmem, hbm, hbm],
        out_specs=[vmem, vmem, vmem],
        scratch_shapes=[
            pltpu.VMEM((2, 4, 2 * BLK, HD), BF16),
            pltpu.VMEM((4, 4, 2 * BLK, HD), BF16),
            pltpu.VMEM((4, 16, 2 * BLK, HD), BF16),
            pltpu.VMEM((4, UNIT, HD), BF16),
            pltpu.VMEM((4, UNIT, HD), BF16),
            pltpu.VMEM((4, 2, SPAN, HD), BF16),
            pltpu.VMEM((2, HD, 2 * SPAN), BF16),
            pltpu.VMEM((4, KEYS, UNIT), F32),
            pltpu.VMEM((4, KEYS, UNIT), F32),
            pltpu.VMEM((4, 2, NT // 2, UNIT), F32),
            pltpu.VMEM((4, 8, UNIT), F32),
            pltpu.VMEM((4, 8, 16, HD), F32),
            pltpu.VMEM((4, 1, UNIT), F32),
            pltpu.VMEM((KEYS, HD), F32),
            pltpu.VMEM((KEYS, HD), F32),
            pltpu.VMEM((4, UNIT, HD), F32),
            pltpu.VMEM((4, 4, 4 * BLK, HD), BF16),
            pltpu.VMEM((4, 4, 4 * BLK, HD), BF16),
            pltpu.VMEM((4, 4, BLK + 8, HD), BF16),
            pltpu.VMEM((16, BLK + 8, HD), BF16),
            pltpu.VMEM((2, 2, SPAN, HD), BF16),
            pltpu.VMEM((2, 2, SPAN, HD), BF16),
            pltpu.VMEM((2, SPAN, HD), BF16),
            pltpu.VMEM((2, SPAN, HD), BF16),
            dma((2,)),
            dma((4, 2)),
            dma((4, 2)),
            dma((4,)),
            dma((4,)),
            dma((4,)),
            dma((4,)),
            dma((4,)),
            dma((4,)),
            dma((4,)),
            dma((4,)),
            dma((4,)),
            dma((4,)),
            dma((2, 2)),
            dma((2,)),
        ],
        compiler_params=pltpu.CompilerParams(
            collective_id=0, has_side_effects=True, vmem_limit_bytes=60 * 2**20
        ),
        name="window_grads",
    )(prompt_len, resp_len, queries, grad_out, keys, values)


def solution(mesh):
    in_specs = (
        P(("group", "ctx"), None),
        P(("group", "ctx"), None),
        P("ctx", None),
        P("ctx", None),
        P(),
        P("group", None),
    )
    out_specs = (P(("group", "ctx"), None), P("ctx", "group"), P("ctx", "group"))
    return jax.shard_map(
        on_device, mesh=mesh, in_specs=in_specs, out_specs=out_specs, check_vma=False
    )
```

time: 74.5 us -> 65.8 us (0.88)
  the two profiles are of different devices: /device:TPU:38 before, /device:TPU:1 now
where the time goes in v2:
time: 65.8 us; the launch traced here: 65.7 us
  Pallas kernels  61.2 us (93%)
  local copies, waits for them, and re-layouts  3.17 us (5%)
  between operations  1.3 us (2%)
    pallas_call x1, Pallas kernels, on_device(): pl.pallas_call(kernel, out_shape=[jax.ShapeDtypeStruct((OWN, QH * HD), BF...  61.2 us
    unnamed x7, local copies, waits for them, and re-layouts  3.17 us

profile of v2, /device:TPU:1, one launch (start us, length us, event | category | flops | bytes accessed | tf_op | source)
XLA Modules:
  0.0 65.7 jit_solution(15716357805819983161)
XLA Ops:
  1.3 61.2 %window_grads.1 = (bf16[8,5120]{1,0:T(8,128)(2,1)}, bf16[512,128]{1,0:T(8,128)(2,1)}, bf16[512,128]{1,0:T(8,128)(2,1)}) custom-call(s32[1]{0:T(128)S(6)} %copy.12.plen_ref, s32[1,2]{1,0:T(1,128)} %rlen_ref.1, bf16[8,5120]{1,0:T(8,128)(2,1)} %q_ref.1, bf16[8,5120]{1,0:T(8,128)(2,1)} %do_ref.1, bf16[512,1024]{1,0:T(8,128)(2,1)} %k_hbm.1, bf16[512,1024]{1,0:T(8,128)(2,1)} %v_hbm.1), custom_call_target="tpu_custom_call" | custom-call | tf_op jit(solution)/shard_map/window_grads/pallas_call | solution.py:435
  62.5 0.0 copy-start.1
  62.5 1.6 %copy.13 = bf16[8,5120]{1,0:T(8,128)(2,1)} copy(bf16[8,5120]{1,0:T(8,128)(2,1)} %get-tuple-element.6) | data formatting | bytes 163840
  64.1 0.0 copy-done.1
  64.1 0.0 copy-start
  64.1 0.7 copy.14
  64.7 0.3 copy-done
  65.0 0.7 copy.15
Async XLA Ops:
  62.5 1.6 %copy-start.1 = (bf16[512,128]{1,0:T(8,128)(2,1)S(1)}, bf16[512,128]{1,0:T(8,128)(2,1)}, u32[]{:S(2)}) copy-start(bf16[512,128]{1,0:T(8,128)(2,1)} %get-tuple-element.7) | copy-start | bytes 393220
  64.1 1.0 %copy-start = (bf16[512,128]{1,0:T(8,128)(2,1)S(1)}, bf16[512,128]{1,0:T(8,128)(2,1)}, u32[]{:S(2)}) copy-start(bf16[512,128]{1,0:T(8,128)(2,1)} %get-tuple-element.8) | copy-start | bytes 393220

commit v3 on v2

--- a/solution.py
+++ b/solution.py
@@ -45,10 +45,10 @@
 
 
 def kernel(
-    plen_ref, rlen_ref, q_ref, do_ref, k_hbm, v_hbm,
-    dq_ref, dk_ref, dv_ref,
-    snd, held, gath, q_s, do_s, kv, k_t, e_buf, dp_buf, mst, st_loc, st_all, rdots, dka, dva, dq_acc,
-    r_out, r_in, f_out, f_in, c_out, c_in, zz_out, zz_in,
+    plen_ref, rlen_ref, q_hbm, do_hbm, k_hbm, v_hbm,
+    f_in, dk_ref, dv_ref,
+    q_ref, do_ref, snd, held, gath, q_s, do_s, kv, k_t, e_buf, dp_buf, mst, st_loc, st_all, rdots, dka, dva, dq_acc,
+    r_out, r_in, f_out, c_out, c_in, zz_out, zz_in,
     loc_sem, kv_send, kv_recv, z_send, z_recv, g_send, g_recv, st_send, st_recv,
     r_send, r_recv, f_send, f_recv, c_sem, zz_sem,
 ):
@@ -101,6 +101,10 @@
     def level(k):
         return (((y + k) % 4) * 2 + z_hi, ctx_of((x + k // 4) % 4, z_lo, core))
 
+    loads = [pltpu.make_async_copy(a, b, loc_sem.at[2 + i]) for i, (a, b) in enumerate(((q_hbm, q_ref), (do_hbm, do_ref)))]
+    for cp in loads:
+        cp.start()
+
     barrier = pltpu.get_barrier_semaphore()
 
     def greet(dev):
@@ -120,6 +124,8 @@
     for cp in local:
         cp.start()
 
+    for cp in loads:
+        cp.wait()
     qf = q_ref[...].astype(F32)
     live_to = rlen_ref[0, c // 16]
     t_row = (c % 16) * OWN + lax.broadcasted_iota(jnp.int32, (OWN, 1), 0)
@@ -132,9 +138,11 @@
     pl.semaphore_wait(barrier, 32)
 
     def z_copy(r):
-        dest = order[r]
+        if r == 3:
+            part = held.at[order[2]]
+            return remote(part, part, z_send.at[3], z_recv.at[3], mate)
         half = z_hi if r == 1 else 1 - z_hi
-        return remote(snd.at[half], held.at[zq], z_send.at[r], z_recv.at[r], place(dest * 4 + y))
+        return remote(snd.at[half], held.at[zq], z_send.at[r], z_recv.at[r], place(order[r] * 4 + y))
 
     def g_copy(r, k):
         zr = order[r]
@@ -145,6 +153,8 @@
     def spread(r):
         if r > 0:
             z_copy(r).wait_recv()
+            if r == 2:
+                z_copy(3).start()
             gath[order[r], x * 4 + y] = held[order[r], y]
         repeat(1, 16, lambda k: g_copy(r, k).start())
 
@@ -155,28 +165,30 @@
     z_copy(1).start()
     z_copy(2).start()
     spread(0)
-    z_copy(3).start()
 
     def kv_copy(i, src, slot, dev):
         return remote(src, kv.at[slot, i], kv_send.at[slot, i], kv_recv.at[slot, i], dev)
 
     for i, h in enumerate((k_hbm, v_hbm)):
         kv_copy(i, h.at[:, cols], 1, sib).start()
+        kv_copy(i, h.at[:, cols], 2, zp).start()
 
     dka[...] = jnp.zeros_like(dka)
     dva[...] = jnp.zeros_like(dva)
-    dq_acc[...] = jnp.zeros_like(dq_acc)
     st_loc[...] = jnp.concatenate([jnp.full((4, 1, UNIT), -1e30, F32), jnp.zeros((4, 7, UNIT), F32)], axis=1)
 
     spread(1)
-    for i, h in enumerate((k_hbm, v_hbm)):
-        kv_copy(i, h.at[:, cols], 2, zp).start()
     spread(2)
     for cp in local:
         cp.wait()
     for i in range(2):
         kv_copy(i, kv.at[1, i], 1, sib).wait_recv()
 
+    def turn(slot):
+        k_t[slot // 2, :, slot % 2 * SPAN : (slot % 2 + 1) * SPAN] = kv[slot, 0].astype(F32).T.astype(BF16)
+
+    turn(0)
+    turn(1)
     plen = plen_ref[0]
     c_zp = zp[1]
     c_base = [c * SPAN, sib[1] * SPAN, c_zp * SPAN, (c_zp + 1 - 2 * core) * SPAN]
@@ -196,29 +208,30 @@
         return same * 2 + (1 - r // 2) * mine + (r // 2) * (1 - mine)
 
     def phase1(i, carry):
-        unit = source(jnp.where(i < 6, i % 3, 3))
-        half = jnp.where(i < 6, i // 3, i - 6)
+        unit, half = source(i // 2), i % 2
 
         @pl.when(i == 0)
         def _():
             all15(0).wait_recv()
 
         @pl.when(i == 1)
-        def _():
-            spread(3)
-            all15(1).wait_recv()
-
-        @pl.when(i == 2)
         def _():
             for i_ in range(2):
                 kv_copy(i_, kv.at[2, i_], 2, zp).wait_recv()
                 kv_copy(i_, kv.at[2, i_], 3, sib).start()
-            all15(2).wait_recv()
-
-        @pl.when(i == 3)
-        def _():
+            spread(3)
+            turn(2)
             for i_ in range(2):
                 kv_copy(i_, kv.at[3, i_], 3, sib).wait_recv()
+            turn(3)
+
+        @pl.when(i == 2)
+        def _():
+            all15(1).wait_recv()
+
+        @pl.when(i == 4)
+        def _():
+            all15(2).wait_recv()
 
         @pl.when(i == 6)
         def _():
@@ -282,9 +295,6 @@
 
     lax.fori_loop(0, 8, phase1, 0)
 
-    for slot in range(4):
-        k_t[slot // 2, :, slot % 2 * SPAN : (slot % 2 + 1) * SPAN] = kv[slot, 0].astype(F32).T.astype(BF16)
-
     def combine(unit):
         st_seven(unit).wait_recv()
         stats = st_all[unit]
@@ -309,7 +319,7 @@
         return remote(part, part, r_send.at[r], r_recv.at[r], at_x(1))
 
     def scatter(r):
-        dq = dq_acc[order[r]]
+        dq = dq_acc[source(r)]
         for n in range(4):
             r_out[r, n] = dq[n * 4 * BLK : (n + 1) * 4 * BLK].astype(BF16)
         for k in (1, 2, 3):
@@ -342,64 +352,58 @@
         c_out[n, 1] = dva[rows].astype(BF16)
         c_copy[n].start()
 
-    def phase2(i, carry):
-        r = jnp.where(i < 3, 1 - i % 2, jnp.where(i < 7, 2 + (i // 4) * (1 - i // 6), 0))
+    def q_step(n):
+        r = n + 1 - 2 * (n % 2)
         unit = source(r)
-        half = jnp.where(i < 5, 1 - (i // 2) * (1 - i // 3), 0)
-
-        @pl.when(i < 2)
-        def _():
-            combine(unit)
-
-        @pl.when((i == 3) | (i == 4))
-        def _():
-            combine(unit)
-
-        def cell():
-            qu, dou = q_s[unit], do_s[unit]
-            factor, rdot = mst[unit, half], rdots[unit]
-            dq_t = jnp.zeros((HD, UNIT), F32)
-            for t in range(NT // 2):
-                rows = pl.ds(pl.multiple_of(half * 2 * SPAN + t * KT, KT), KT)
-                p = e_buf[unit, rows] * factor[t : t + 1]
-                ds = (p * (dp_buf[unit, rows] - rdot)).astype(BF16)
-                dva[rows] += dot(p.astype(BF16), dou)
-                dka[rows] += dot(ds, qu)
-                dq_t += dot(k_t[half, :, t * KT : (t + 1) * KT], ds)
-            dq_acc[unit] += dq_t.T * SCALE
-
-        cell()
-
-        @pl.when(i == 2)
-        def _():
-            scatter(1)
-
-        @pl.when(i == 4)
-        def _():
-            c_start(1)
-
-        @pl.when(i == 5)
-        def _():
-            scatter(3)
+        combine(unit)
+        rdot = rdots[unit]
+        dq_t = jnp.zeros((HD, UNIT), F32)
+        for t in range(NT):
+            rows = pl.ds(t * KT, KT)
+            p = e_buf[unit, rows] * mst[unit, t // 4, t % 4 : t % 4 + 1]
+            ds = p * (dp_buf[unit, rows] - rdot)
+            dp_buf[unit, rows] = ds
+            dq_t += dot(k_t[t // 4, :, t % 4 * KT : (t % 4 + 1) * KT], ds.astype(BF16))
+        dq_acc[unit] = dq_t.T * SCALE
+        scatter(r)
+
+    def kv_step(unit, half):
+        qu, dou, factor = q_s[unit], do_s[unit], mst[unit, half]
+        for t in range(NT // 2):
+            rows = pl.ds(half * 2 * SPAN + t * KT, KT)
+            p = (e_buf[unit, rows] * factor[t : t + 1]).astype(BF16)
+            dva[rows] += dot(p, dou)
+            dka[rows] += dot(dp_buf[unit, rows].astype(BF16), qu)
+
+    repeat(0, 2, q_step)
+    repeat(0, 2, lambda n: kv_step(source(n), 1))
+    repeat(2, 4, q_step)
+    deliver(1)
+    deliver(0)
+    repeat(2, 4, lambda n: kv_step(source(n), 1))
+    c_start(1)
+
+    def near_step(n):
+        kv_step(source(n), 0)
+
+        @pl.when(n == 0)
+        def _():
             c_copy[1].wait_recv()
             far = pl.ds(2 * SPAN, SPAN)
             zz_out[0] = (dka[far] * SCALE + c_in[1, 0].astype(F32)).astype(BF16)
             zz_out[1] = (dva[far] + c_in[1, 1].astype(F32)).astype(BF16)
+
+        @pl.when(n == 1)
+        def _():
+            deliver(3)
+
+        @pl.when(n == 2)
+        def _():
+            deliver(2)
             zz_copy.start()
 
-        @pl.when(i == 6)
-        def _():
-            scatter(2)
-            deliver(1)
-
-        return carry
-
-    lax.fori_loop(0, 8, phase2, 0)
-    scatter(0)
+    repeat(0, 4, near_step)
     c_start(0)
-    deliver(3)
-    deliver(2)
-    deliver(0)
 
     c_copy[0].wait_recv()
     near = pl.ds(0, SPAN)
@@ -411,12 +415,6 @@
 
     for r in range(4):
         f_part(r).wait_recv()
-    out = []
-    for b in range(KH):
-        first = (b % 2) * 8 + b // 2
-        blk = f_in[first].astype(F32) + f_in[first + 4].astype(F32)
-        out += [blk[a * OWN : (a + 1) * OWN] for a in range(SHARE)]
-    dq_ref[...] = jnp.concatenate(out, axis=1).astype(BF16)
 
     drain_a()
     for n in range(2):
@@ -427,21 +425,34 @@
         f_part(r).wait_send()
 
 
+def assemble(f_ref, dk_in, dv_in, dq_ref, dk_ref, dv_ref):
+    out = []
+    for b in range(KH):
+        first = (b % 2) * 8 + b // 2
+        blk = f_ref[first].astype(F32) + f_ref[first + 4].astype(F32)
+        out += [blk[a * OWN : (a + 1) * OWN] for a in range(SHARE)]
+    dq_ref[...] = jnp.concatenate(out, axis=1).astype(BF16)
+    dk_ref[...] = dk_in[...]
+    dv_ref[...] = dv_in[...]
+
+
 def on_device(queries, grad_out, keys, values, prompt_len, resp_len):
     vmem = pl.BlockSpec(memory_space=pltpu.VMEM)
     smem = pl.BlockSpec(memory_space=pltpu.SMEM)
     hbm = pl.BlockSpec(memory_space=pl.ANY)
     dma = pltpu.SemaphoreType.DMA
-    return pl.pallas_call(
+    parts = pl.pallas_call(
         kernel,
         out_shape=[
-            jax.ShapeDtypeStruct((OWN, QH * HD), BF16),
+            jax.ShapeDtypeStruct((16, BLK + 8, HD), BF16),
             jax.ShapeDtypeStruct((SPAN, HD), BF16),
             jax.ShapeDtypeStruct((SPAN, HD), BF16),
         ],
-        in_specs=[smem, smem, vmem, vmem, hbm, hbm],
+        in_specs=[smem, smem, hbm, hbm, hbm, hbm],
         out_specs=[vmem, vmem, vmem],
         scratch_shapes=[
+            pltpu.VMEM((OWN, QH * HD), BF16),
+            pltpu.VMEM((OWN, QH * HD), BF16),
             pltpu.VMEM((2, 4, 2 * BLK, HD), BF16),
             pltpu.VMEM((4, 4, 2 * BLK, HD), BF16),
             pltpu.VMEM((4, 16, 2 * BLK, HD), BF16),
@@ -461,12 +472,11 @@
             pltpu.VMEM((4, 4, 4 * BLK, HD), BF16),
             pltpu.VMEM((4, 4, 4 * BLK, HD), BF16),
             pltpu.VMEM((4, 4, BLK + 8, HD), BF16),
-            pltpu.VMEM((16, BLK + 8, HD), BF16),
             pltpu.VMEM((2, 2, SPAN, HD), BF16),
             pltpu.VMEM((2, 2, SPAN, HD), BF16),
             pltpu.VMEM((2, SPAN, HD), BF16),
             pltpu.VMEM((2, SPAN, HD), BF16),
-            dma((2,)),
+            dma((4,)),
             dma((4, 2)),
             dma((4, 2)),
             dma((4,)),
@@ -487,6 +497,17 @@
         ),
         name="window_grads",
     )(prompt_len, resp_len, queries, grad_out, keys, values)
+    return pl.pallas_call(
+        assemble,
+        out_shape=[
+            jax.ShapeDtypeStruct((OWN, QH * HD), BF16),
+            jax.ShapeDtypeStruct((SPAN, HD), BF16),
+            jax.ShapeDtypeStruct((SPAN, HD), BF16),
+        ],
+        in_specs=[vmem] * 3,
+        out_specs=[vmem] * 3,
+        name="assemble",
+    )(*parts)
 
 
 def solution(mesh):

time: 65.8 us -> 62.4 us (0.948)
  local copies, waits for them, and re-layouts: 3.17 us -> 0 us
    unnamed x7 -> x0, local copies, waits for them, and re-layouts: 3.17 us -> none
    pallas_call x1 -> x2, Pallas kernels: 61.2 us -> 61 us  [the longest x1 59.2 us: on_device(): pl.pallas_call(kernel, out_shape=[jax.ShapeDtypeStruct((16, BLK + 8, HD),...]
where the time goes in v3:
time: 62.4 us; the launch traced here: 62.3 us
  Pallas kernels  61 us (98%)
  between operations  1.29 us (2%)
    pallas_call x1, Pallas kernels, on_device(): pl.pallas_call(kernel, out_shape=[jax.ShapeDtypeStruct((16, BLK + 8, HD),...  59.2 us
    pallas_call x1, Pallas kernels, on_device(): pl.pallas_call(assemble, out_shape=[jax.ShapeDtypeStruct((OWN, QH * HD),...  1.8 us

profile of v3, /device:TPU:1, one launch (start us, length us, event | category | flops | bytes accessed | tf_op | source)
XLA Modules:
  0.0 62.3 jit_solution(11201345174245300390)
XLA Ops:
  1.3 59.2 %window_grads.1 = (bf16[16,48,128]{2,1,0:T(8,128)(2,1)}, bf16[512,128]{1,0:T(8,128)(2,1)}, bf16[512,128]{1,0:T(8,128)(2,1)}) custom-call(s32[1]{0:T(128)S(6)} %copy.9.plen_ref, s32[1,2]{1,0:T(1,128)} %rlen_ref.1, bf16[8,5120]{1,0:T(8,128)(2,1)} %q_hbm.1, bf16[8,5120]{1,0:T(8,128)(2,1)} %do_hbm.1, bf16[512,1024]{1,0:T(8,128)(2,1)} %k_hbm.1, ...), custom_call_target="tpu_custom_call" | custom-call | tf_op jit(solution)/shard_map/window_grads/pallas_call | solution.py:444
  60.5 1.8 %assemble.1 = (bf16[8,5120]{1,0:T(8,128)(2,1)}, bf16[512,128]{1,0:T(8,128)(2,1)}, bf16[512,128]{1,0:T(8,128)(2,1)}) custom-call(bf16[16,48,128]{2,1,0:T(8,128)(2,1)} %get-tuple-element.6.f_ref, bf16[512,128]{1,0:T(8,128)(2,1)} %get-tuple-element.7.dk_in, bf16[512,128]{1,0:T(8,128)(2,1)} %get-tuple-element.8.dv_in), custom_call_target="tpu_custom_call" | custom-call | tf_op jit(solution)/shard_map/assemble/pallas_call | solution.py:500

commit v4 on v3

--- a/solution.py
+++ b/solution.py
@@ -46,9 +46,9 @@
 
 def kernel(
     plen_ref, rlen_ref, q_hbm, do_hbm, k_hbm, v_hbm,
-    f_in, dk_ref, dv_ref,
+    f_in, dk_hbm, dv_hbm,
     q_ref, do_ref, snd, held, gath, q_s, do_s, kv, k_t, e_buf, dp_buf, mst, st_loc, st_all, rdots, dka, dva, dq_acc,
-    r_out, r_in, f_out, c_out, c_in, zz_out, zz_in,
+    r_out, r_in, f_out, c_out, c_in, zz_out, zz_in, done,
     loc_sem, kv_send, kv_recv, z_send, z_recv, g_send, g_recv, st_send, st_recv,
     r_send, r_recv, f_send, f_recv, c_sem, zz_sem,
 ):
@@ -137,33 +137,39 @@
 
     pl.semaphore_wait(barrier, 32)
 
-    def z_copy(r):
+    def z_copy(r, j):
+        head = (y + j) % 4
         if r == 3:
-            part = held.at[order[2]]
-            return remote(part, part, z_send.at[3], z_recv.at[3], mate)
+            part = held.at[order[2], head]
+            return remote(part, part, z_send.at[3, head], z_recv.at[3, head], mate)
         half = z_hi if r == 1 else 1 - z_hi
-        return remote(snd.at[half], held.at[zq], z_send.at[r], z_recv.at[r], place(order[r] * 4 + y))
-
-    def g_copy(r, k):
+        dev = place(order[r] * 4 + y)
+        return remote(snd.at[half, head], held.at[zq, head], z_send.at[r, head], z_recv.at[r, head], dev)
+
+    def g_copy(r, j, dx):
         zr = order[r]
-        head = (y + k) % 4
+        head = (y + j) % 4
         src = snd.at[z_hi, head] if r == 0 else held.at[zr, head]
-        return remote(src, gath.at[zr, x * 4 + y], g_send.at[r], g_recv.at[r], level(k))
+        return remote(src, gath.at[zr, x * 4 + y], g_send.at[r], g_recv.at[r], level(dx * 4 + j))
 
     def spread(r):
-        if r > 0:
-            z_copy(r).wait_recv()
+        for j in range(4):
+            if r > 0:
+                z_copy(r, j).wait_recv()
             if r == 2:
-                z_copy(3).start()
-            gath[order[r], x * 4 + y] = held[order[r], y]
-        repeat(1, 16, lambda k: g_copy(r, k).start())
+                z_copy(3, j).start()
+            if r > 0 and j == 0:
+                gath[order[r], x * 4 + y] = held[order[r], y]
+            repeat(1 if j == 0 else 0, 4, lambda dx: g_copy(r, j, dx).start())
 
     def all15(r):
         part = gath.at[order[r], pl.ds(0, 15)]
         return remote(part, part, g_send.at[r], g_recv.at[r], level(1))
 
-    z_copy(1).start()
-    z_copy(2).start()
+    for j in range(4):
+        z_copy(1, j).start()
+    for j in range(4):
+        z_copy(2, j).start()
     spread(0)
 
     def kv_copy(i, src, slot, dev):
@@ -286,7 +292,8 @@
         for r in range(4):
             all15(r).wait_send()
         for r in (1, 2, 3):
-            z_copy(r).wait_send()
+            for j in range(4):
+                z_copy(r, j).wait_send()
         for i in range(2):
             kv_copy(i, kv.at[2, i], 2, zp).wait_send()
             kv_copy(i, kv.at[1, i], 1, sib).wait_send()
@@ -308,7 +315,7 @@
 
 
     c_copy = [remote(c_out.at[n], c_in.at[n], c_sem.at[0, n], c_sem.at[1, n], sib) for n in range(2)]
-    zz_copy = remote(zz_out, zz_in, zz_sem.at[0], zz_sem.at[1], zp)
+    zz_copy = [remote(zz_out.at[i], zz_in.at[i], zz_sem.at[0, i], zz_sem.at[1, i], zp) for i in range(2)]
 
     def r_copy(r, k):
         dest = (x + k) % 4
@@ -333,6 +340,8 @@
         count = 3 if r == 0 else 4
         part = f_in.at[pl.ds(0, count)]
         return remote(part, part, f_send.at[r], f_recv.at[r], place(order[r] * 4 + y))
+
+    keep = pltpu.make_async_copy(f_out.at[0, y], f_in.at[me16], loc_sem.at[0])
 
     def deliver(r):
         r_three(r).wait_recv()
@@ -343,7 +352,7 @@
         for n in range(4):
             f_out[r, n] = jnp.concatenate([tot[n * BLK : (n + 1) * BLK], pad], axis=0).astype(BF16)
         if r == 0:
-            f_in[me16] = f_out[0, y]
+            keep.start()
         repeat(1 if r == 0 else 0, 4, lambda k: f_copy(r, k).start())
 
     def c_start(n):
@@ -378,10 +387,10 @@
     repeat(0, 2, q_step)
     repeat(0, 2, lambda n: kv_step(source(n), 1))
     repeat(2, 4, q_step)
+    repeat(2, 4, lambda n: kv_step(source(n), 1))
+    c_start(1)
     deliver(1)
     deliver(0)
-    repeat(2, 4, lambda n: kv_step(source(n), 1))
-    c_start(1)
 
     def near_step(n):
         kv_step(source(n), 0)
@@ -396,11 +405,12 @@
         @pl.when(n == 1)
         def _():
             deliver(3)
+            zz_copy[0].start()
 
         @pl.when(n == 2)
         def _():
             deliver(2)
-            zz_copy.start()
+            zz_copy[1].start()
 
     repeat(0, 4, near_step)
     c_start(0)
@@ -409,17 +419,24 @@
     near = pl.ds(0, SPAN)
     dka[near] = dka[near] * SCALE + c_in[0, 0].astype(F32)
     dva[near] = dva[near] + c_in[0, 1].astype(F32)
-    zz_copy.wait_recv()
-    dk_ref[...] = (dka[near] + zz_in[0].astype(F32)).astype(BF16)
-    dv_ref[...] = (dva[near] + zz_in[1].astype(F32)).astype(BF16)
+    stores = []
+    for i, (near_sum, out) in enumerate(((dka, dk_hbm), (dva, dv_hbm))):
+        zz_copy[i].wait_recv()
+        done[i] = (near_sum[near] + zz_in[i].astype(F32)).astype(BF16)
+        stores.append(pltpu.make_async_copy(done.at[i], out, loc_sem.at[1 + i]))
+        stores[i].start()
 
     for r in range(4):
         f_part(r).wait_recv()
 
+    keep.wait()
+    for store in stores:
+        store.wait()
     drain_a()
     for n in range(2):
         c_copy[n].wait_send()
-    zz_copy.wait_send()
+    for i in range(2):
+        zz_copy[i].wait_send()
     for r in range(4):
         r_three(r).wait_send()
         f_part(r).wait_send()
@@ -449,7 +466,7 @@
             jax.ShapeDtypeStruct((SPAN, HD), BF16),
         ],
         in_specs=[smem, smem, hbm, hbm, hbm, hbm],
-        out_specs=[vmem, vmem, vmem],
+        out_specs=[hbm, hbm, hbm],
         scratch_shapes=[
             pltpu.VMEM((OWN, QH * HD), BF16),
             pltpu.VMEM((OWN, QH * HD), BF16),
@@ -476,11 +493,12 @@
             pltpu.VMEM((2, 2, SPAN, HD), BF16),
             pltpu.VMEM((2, SPAN, HD), BF16),
             pltpu.VMEM((2, SPAN, HD), BF16),
+            pltpu.VMEM((2, SPAN, HD), BF16),
             dma((4,)),
             dma((4, 2)),
             dma((4, 2)),
-            dma((4,)),
-            dma((4,)),
+            dma((4, 4)),
+            dma((4, 4)),
             dma((4,)),
             dma((4,)),
             dma((4,)),
@@ -490,7 +508,7 @@
             dma((4,)),
             dma((4,)),
             dma((2, 2)),
-            dma((2,)),
+            dma((2, 2)),
         ],
         compiler_params=pltpu.CompilerParams(
             collective_id=0, has_side_effects=True, vmem_limit_bytes=60 * 2**20

time: 62.4 us -> 60.2 us (0.965)
  Pallas kernels: 61 us -> 58.8 us
    pallas_call x1, Pallas kernels: 59.2 us -> 57 us  [on_device(): pl.pallas_call(kernel, out_shape=[jax.ShapeDtypeStruct((16, BLK + 8, HD),...]
where the time goes in v4:
time: 60.2 us; the launch traced here: 60.1 us
  Pallas kernels  58.8 us (98%)
  between operations  1.29 us (2%)
    pallas_call x1, Pallas kernels, on_device(): pl.pallas_call(kernel, out_shape=[jax.ShapeDtypeStruct((16, BLK + 8, HD),...  57 us
    pallas_call x1, Pallas kernels, on_device(): pl.pallas_call(assemble, out_shape=[jax.ShapeDtypeStruct((OWN, QH * HD),...  1.8 us

profile of v4, /device:TPU:1, one launch (start us, length us, event | category | flops | bytes accessed | tf_op | source)
XLA Modules:
  0.0 60.1 jit_solution(7668209767764181536)
XLA Ops:
  1.3 57.0 %window_grads.1 = (bf16[16,48,128]{2,1,0:T(8,128)(2,1)}, bf16[512,128]{1,0:T(8,128)(2,1)}, bf16[512,128]{1,0:T(8,128)(2,1)}) custom-call(s32[1]{0:T(128)S(6)} %copy.9.plen_ref, s32[1,2]{1,0:T(1,128)} %rlen_ref.1, bf16[8,5120]{1,0:T(8,128)(2,1)} %q_hbm.1, bf16[8,5120]{1,0:T(8,128)(2,1)} %do_hbm.1, bf16[512,1024]{1,0:T(8,128)(2,1)} %k_hbm.1, ...), custom_call_target="tpu_custom_call" | custom-call | tf_op jit(solution)/shard_map/window_grads/pallas_call | solution.py:461
  58.3 1.8 %assemble.1 = (bf16[8,5120]{1,0:T(8,128)(2,1)}, bf16[512,128]{1,0:T(8,128)(2,1)}, bf16[512,128]{1,0:T(8,128)(2,1)}) custom-call(bf16[16,48,128]{2,1,0:T(8,128)(2,1)} %get-tuple-element.6.f_ref, bf16[512,128]{1,0:T(8,128)(2,1)} %get-tuple-element.7.dk_in, bf16[512,128]{1,0:T(8,128)(2,1)} %get-tuple-element.8.dv_in), custom_call_target="tpu_custom_call" | custom-call | tf_op jit(solution)/shard_map/assemble/pallas_call | solution.py:518

commit v5 on v4

--- a/solution.py
+++ b/solution.py
@@ -314,7 +314,10 @@
         mst[unit] = jnp.exp2((mst[unit] - top[None]) * LOG2) * inv[None]
 
 
-    c_copy = [remote(c_out.at[n], c_in.at[n], c_sem.at[0, n], c_sem.at[1, n], sib) for n in range(2)]
+    c_copy = [
+        [remote(c_out.at[n, i], c_in.at[n, i], c_sem.at[0, n, i], c_sem.at[1, n, i], sib) for i in range(2)]
+        for n in range(2)
+    ]
     zz_copy = [remote(zz_out.at[i], zz_in.at[i], zz_sem.at[0, i], zz_sem.at[1, i], zp) for i in range(2)]
 
     def r_copy(r, k):
@@ -355,11 +358,16 @@
             keep.start()
         repeat(1 if r == 0 else 0, 4, lambda k: f_copy(r, k).start())
 
-    def c_start(n):
+    def c_start(n, i):
         rows = pl.ds((1 + 2 * n) * SPAN, SPAN)
-        c_out[n, 0] = (dka[rows] * SCALE).astype(BF16)
-        c_out[n, 1] = dva[rows].astype(BF16)
-        c_copy[n].start()
+        c_out[n, i] = (dka[rows] * SCALE if i == 0 else dva[rows]).astype(BF16)
+        c_copy[n][i].start()
+
+    def zz_make(i):
+        c_copy[1][i].wait_recv()
+        far = pl.ds(2 * SPAN, SPAN)
+        mine = dka[far] * SCALE if i == 0 else dva[far]
+        zz_out[i] = (mine + c_in[1, i].astype(F32)).astype(BF16)
 
     def q_step(n):
         r = n + 1 - 2 * (n % 2)
@@ -376,46 +384,46 @@
         dq_acc[unit] = dq_t.T * SCALE
         scatter(r)
 
-    def kv_step(unit, half):
+    def kv_step(unit, half, key=True, value=True):
         qu, dou, factor = q_s[unit], do_s[unit], mst[unit, half]
         for t in range(NT // 2):
             rows = pl.ds(half * 2 * SPAN + t * KT, KT)
-            p = (e_buf[unit, rows] * factor[t : t + 1]).astype(BF16)
-            dva[rows] += dot(p, dou)
-            dka[rows] += dot(dp_buf[unit, rows].astype(BF16), qu)
+            if value:
+                dva[rows] += dot((e_buf[unit, rows] * factor[t : t + 1]).astype(BF16), dou)
+            if key:
+                dka[rows] += dot(dp_buf[unit, rows].astype(BF16), qu)
 
     repeat(0, 2, q_step)
     repeat(0, 2, lambda n: kv_step(source(n), 1))
     repeat(2, 4, q_step)
-    repeat(2, 4, lambda n: kv_step(source(n), 1))
-    c_start(1)
+    repeat(2, 4, lambda n: kv_step(source(n), 1, key=False))
+    c_start(1, 1)
+    repeat(2, 4, lambda n: kv_step(source(n), 1, value=False))
+    c_start(1, 0)
     deliver(1)
     deliver(0)
+    zz_make(1)
+    zz_copy[1].start()
 
     def near_step(n):
         kv_step(source(n), 0)
 
         @pl.when(n == 0)
         def _():
-            c_copy[1].wait_recv()
-            far = pl.ds(2 * SPAN, SPAN)
-            zz_out[0] = (dka[far] * SCALE + c_in[1, 0].astype(F32)).astype(BF16)
-            zz_out[1] = (dva[far] + c_in[1, 1].astype(F32)).astype(BF16)
-
-        @pl.when(n == 1)
-        def _():
+            zz_make(0)
             deliver(3)
+
+        @pl.when(n == 2)
+        def _():
+            deliver(2)
             zz_copy[0].start()
 
-        @pl.when(n == 2)
-        def _():
-            deliver(2)
-            zz_copy[1].start()
-
     repeat(0, 4, near_step)
-    c_start(0)
-
-    c_copy[0].wait_recv()
+    c_start(0, 0)
+    c_start(0, 1)
+
+    for i in range(2):
+        c_copy[0][i].wait_recv()
     near = pl.ds(0, SPAN)
     dka[near] = dka[near] * SCALE + c_in[0, 0].astype(F32)
     dva[near] = dva[near] + c_in[0, 1].astype(F32)
@@ -434,7 +442,8 @@
         store.wait()
     drain_a()
     for n in range(2):
-        c_copy[n].wait_send()
+        for i in range(2):
+            c_copy[n][i].wait_send()
     for i in range(2):
         zz_copy[i].wait_send()
     for r in range(4):
@@ -507,7 +516,7 @@
             dma((4,)),
             dma((4,)),
             dma((4,)),
-            dma((2, 2)),
+            dma((2, 2, 2)),
             dma((2, 2)),
         ],
         compiler_params=pltpu.CompilerParams(

time: 60.2 us -> 59.7 us (level)
  no operation moved by 1% of the time
where the time goes in v5:
time: 59.7 us; the launch traced here: 59.6 us
  Pallas kernels  58.3 us (98%)
  between operations  1.29 us (2%)
    pallas_call x1, Pallas kernels, on_device(): pl.pallas_call(kernel, out_shape=[jax.ShapeDtypeStruct((16, BLK + 8, HD),...  56.5 us
    pallas_call x1, Pallas kernels, on_device(): pl.pallas_call(assemble, out_shape=[jax.ShapeDtypeStruct((OWN, QH * HD),...  1.8 us

profile of v5, /device:TPU:1, one launch (start us, length us, event | category | flops | bytes accessed | tf_op | source)
XLA Modules:
  0.0 59.6 jit_solution(12937720460863686223)
XLA Ops:
  1.3 56.5 %window_grads.1 = (bf16[16,48,128]{2,1,0:T(8,128)(2,1)}, bf16[512,128]{1,0:T(8,128)(2,1)}, bf16[512,128]{1,0:T(8,128)(2,1)}) custom-call(s32[1]{0:T(128)S(6)} %copy.9.plen_ref, s32[1,2]{1,0:T(1,128)} %rlen_ref.1, bf16[8,5120]{1,0:T(8,128)(2,1)} %q_hbm.1, bf16[8,5120]{1,0:T(8,128)(2,1)} %do_hbm.1, bf16[512,1024]{1,0:T(8,128)(2,1)} %k_hbm.1, ...), custom_call_target="tpu_custom_call" | custom-call | tf_op jit(solution)/shard_map/window_grads/pallas_call | solution.py:470
  57.8 1.8 %assemble.1 = (bf16[8,5120]{1,0:T(8,128)(2,1)}, bf16[512,128]{1,0:T(8,128)(2,1)}, bf16[512,128]{1,0:T(8,128)(2,1)}) custom-call(bf16[16,48,128]{2,1,0:T(8,128)(2,1)} %get-tuple-element.6.f_ref, bf16[512,128]{1,0:T(8,128)(2,1)} %get-tuple-element.7.dk_in, bf16[512,128]{1,0:T(8,128)(2,1)} %get-tuple-element.8.dv_in), custom_call_target="tpu_custom_call" | custom-call | tf_op jit(solution)/shard_map/assemble/pallas_call | solution.py:527

commit v6 on v5

--- a/solution.py
+++ b/solution.py
@@ -167,9 +167,8 @@
         return remote(part, part, g_send.at[r], g_recv.at[r], level(1))
 
     for j in range(4):
+        z_copy(2, j).start()
         z_copy(1, j).start()
-    for j in range(4):
-        z_copy(2, j).start()
     spread(0)
 
     def kv_copy(i, src, slot, dev):

time: 59.7 us -> 59.7 us (level)
  no operation moved by 1% of the time
where the time goes in v6:
time: 59.7 us; the launch traced here: 59.6 us
  Pallas kernels  58.3 us (98%)
  between operations  1.29 us (2%)
    pallas_call x1, Pallas kernels, on_device(): pl.pallas_call(kernel, out_shape=[jax.ShapeDtypeStruct((16, BLK + 8, HD),...  56.5 us
    pallas_call x1, Pallas kernels, on_device(): pl.pallas_call(assemble, out_shape=[jax.ShapeDtypeStruct((OWN, QH * HD),...  1.8 us

profile of v6, /device:TPU:1, one launch (start us, length us, event | category | flops | bytes accessed | tf_op | source)
XLA Modules:
  0.0 59.6 jit_solution(3417220237058649694)
XLA Ops:
  1.3 56.5 %window_grads.1 = (bf16[16,48,128]{2,1,0:T(8,128)(2,1)}, bf16[512,128]{1,0:T(8,128)(2,1)}, bf16[512,128]{1,0:T(8,128)(2,1)}) custom-call(s32[1]{0:T(128)S(6)} %copy.9.plen_ref, s32[1,2]{1,0:T(1,128)} %rlen_ref.1, bf16[8,5120]{1,0:T(8,128)(2,1)} %q_hbm.1, bf16[8,5120]{1,0:T(8,128)(2,1)} %do_hbm.1, bf16[512,1024]{1,0:T(8,128)(2,1)} %k_hbm.1, ...), custom_call_target="tpu_custom_call" | custom-call | tf_op jit(solution)/shard_map/window_grads/pallas_call | solution.py:469
  57.8 1.8 %assemble.1 = (bf16[8,5120]{1,0:T(8,128)(2,1)}, bf16[512,128]{1,0:T(8,128)(2,1)}, bf16[512,128]{1,0:T(8,128)(2,1)}) custom-call(bf16[16,48,128]{2,1,0:T(8,128)(2,1)} %get-tuple-element.6.f_ref, bf16[512,128]{1,0:T(8,128)(2,1)} %get-tuple-element.7.dk_in, bf16[512,128]{1,0:T(8,128)(2,1)} %get-tuple-element.8.dv_in), custom_call_target="tpu_custom_call" | custom-call | tf_op jit(solution)/shard_map/assemble/pallas_call | solution.py:526
